TPU v7x, 128 devices: a whole 4x4x4 slice. The times are simulated.
128 devices in a mesh: rows: 32 (over y, z, core), mp: 4 (over x).
Axes of the slice: x: 4, y: 4, z: 4, core: 2. Of those that a mesh axis runs over, the one named last changes fastest.
Arguments:
- calib: bfloat16 [2048, 8192], P('rows', 'mp'), may hold values from -40 to 40
- weight: bfloat16 [8192, 8192], P('rows', 'mp'), may hold values from -6 to 6
- inverse_factor: float32 [8192, 8192], P('rows', 'mp'), may hold values from -10 to 12, as said below
- pruned_blocks: int32 [7], replicated, may hold values from 0 to 63, as said below
Outputs:
- pruned_weight: bfloat16 [8192, 8192], P('rows', 'mp')
- next_gram: float32 [8192, 8192], P('rows', 'mp')
Inputs may be any that keep to these rules, and one draw needn't show every extreme that they name: `pruned_blocks`: 7 distinct block numbers in any order; block b holds rows b * 128 to b * 128 + 127. `inverse_factor`: symmetric and positive definite.
All inputs are finite; a program needn't handle non-finite values.
Results may differ from a plain program's by a relative error of at most 0.0095.
Values may be sent and summed in bfloat16 or wider, within the bound.
No kernel may reach another device: no remote copies, remote signals or barrier semaphores. Data moves between devices by JAX's collectives and lax.ppermute only.
A program may use at most 128 MiB of HBM per device.

v0:
```python
import jax
import jax.numpy as jnp
from jax import lax
from jax.sharding import PartitionSpec as P

BLOCK = 128


def spd_solve(chol_lower, right_side):
    forward = lax.linalg.triangular_solve(chol_lower, right_side, left_side=True, lower=True)
    return lax.linalg.triangular_solve(
        chol_lower, forward, left_side=True, lower=True, transpose_a=True
    )


def shards(calib, weight, inverse_factor, pruned_blocks):
    rows_dev = weight.shape[0]
    width_dev = weight.shape[1]
    full_width = width_dev * lax.axis_size("mp")
    row_start = lax.axis_index("rows") * rows_dev
    col_start = lax.axis_index("mp") * width_dev
    starts = pruned_blocks * BLOCK
    block_count = pruned_blocks.shape[0]
    col_pieces = []
    for slot_index in range(block_count):
        offset = starts[slot_index] - col_start
        inside = ((offset >= 0) & (offset < width_dev)).astype(jnp.float32)
        clamped = jnp.clip(offset, 0, width_dev - BLOCK)
        col_pieces.append(lax.dynamic_slice_in_dim(inverse_factor, clamped, BLOCK, 1) * inside)
    columns = lax.psum(jnp.concatenate(col_pieces, axis=1), "mp")
    weight_parts = []
    inverse_parts = []
    for slot_index in range(block_count):
        offset = starts[slot_index] - row_start
        inside = ((offset >= 0) & (offset < rows_dev)).astype(jnp.float32)
        clamped = jnp.clip(offset, 0, rows_dev - BLOCK)
        weight_parts.append(
            lax.dynamic_slice_in_dim(weight, clamped, BLOCK, 0).astype(jnp.float32) * inside
        )
        inverse_parts.append(lax.dynamic_slice_in_dim(columns, clamped, BLOCK, 0) * inside)
    kept_rows = lax.psum(jnp.concatenate(weight_parts, axis=0).astype(jnp.bfloat16), "rows").astype(
        jnp.float32
    )
    inverse_square = lax.psum(jnp.concatenate(inverse_parts, axis=0), "rows")
    chol_lower = jnp.linalg.cholesky(inverse_square)
    solved = spd_solve(chol_lower, kept_rows)
    update = jnp.dot(columns, solved, precision=lax.Precision.HIGHEST)
    block_ids = (row_start + jnp.arange(rows_dev, dtype=jnp.int32)) // BLOCK
    kept_mask = 1.0 - jnp.any(block_ids[:, None] == pruned_blocks[None, :], axis=1).astype(
        jnp.float32
    )
    pruned_weight = ((weight.astype(jnp.float32) - update) * kept_mask[:, None]).astype(
        jnp.bfloat16
    )
    out_scale = float(full_width) ** (-0.5)
    partial_value = lax.dot_general(
        lax.all_gather(calib, "rows", axis=0, tiled=True),
        pruned_weight,
        (((1,), (1,)), ((), ())),
        preferred_element_type=jnp.float32,
    )
    token_count = partial_value.shape[0]
    own_rows = (
        lax.psum_scatter(partial_value, "mp", scatter_dimension=0, tiled=True) * out_scale
    ).astype(jnp.bfloat16)
    gram_term = lax.dot_general(
        own_rows,
        lax.all_gather(own_rows, "rows", axis=1, tiled=True),
        (((0,), (0,)), ((), ())),
        preferred_element_type=jnp.float32,
    )
    gram_block = (
        lax.psum_scatter(
            gram_term.astype(jnp.bfloat16), "mp", scatter_dimension=1, tiled=True
        ).astype(jnp.float32)
        / token_count
    )
    return (pruned_weight, gram_block)


def solution(mesh):
    return jax.shard_map(
        shards,
        mesh=mesh,
        in_specs=(P("rows", "mp"), P("rows", "mp"), P("rows", "mp"), P()),
        out_specs=(P("rows", "mp"), P("rows", "mp")),
        check_vma=False,
    )
```

profile of v0, /device:TPU:1, one launch (start us, length us, event | category | flops | bytes accessed | tf_op | source)
XLA Modules:
  0.0 788.2 jit_solution(16158695444413011221)
XLA Ops:
  28.4 35.7 %all-reduce.5.cloned.1.call-done = f32[256,896]{0,1:T(8,128)} async-done(((f32[256,896]{0,1:T(8,128)}), f32[256,896]{0,1:T(8,128)}) %all-reduce.5.cloned.1.call-update) | async-done | bytes 917520 | tf_op jit(solution)/shard_map/psum | solution.py:30
  72.5 108.5 %all-reduce.9.cloned.1.call-done = bf16[896,2048]{1,0:T(8,128)(2,1)} async-done(((bf16[896,2048]{1,0:T(8,128)(2,1)}), bf16[896,2048]{1,0:T(8,128)(2,1)}) %all-reduce.9.cloned.1.call-update) | async-done | bytes 3670032 | tf_op jit(solution)/shard_map/psum | solution.py:41
  187.0 106.7 %all-reduce.7.cloned.1.call-done = f32[896,896]{0,1:T(8,128)} async-done(((f32[896,896]{0,1:T(8,128)}), f32[896,896]{0,1:T(8,128)}) %all-reduce.7.cloned.1.call-update) | async-done | bytes 3211280 | tf_op jit(solution)/shard_map/psum | solution.py:44
  302.7 11.7 %cholesky.195 = f32[128,128]{1,0:T(8,128)S(1)} custom-call(f32[128,128]{1,0:T(8,128)S(1)} %cholesky.502), custom_call_target="Cholesky" | custom-call | tf_op jit(solution)/shard_map/jit(cholesky)/cholesky | solution.py:45
  314.6 9.8 %custom-call.56 = f32[1,128,128]{1,2,0:T(8,128)S(1)} custom-call(f32[1,128,128]{2,1,0:T(8,128)S(1)} %get-tuple-element.55), custom_call_target="InvertDiagBlocksLowerTriangular" | custom-call | tf_op jit(solution)/shard_map/jit(cholesky)/cholesky | solution.py:45
  328.2 11.7 %cholesky.216 = f32[128,128]{1,0:T(8,128)S(1)} custom-call(f32[128,128]{1,0:T(8,128)S(1)} %cholesky.506), custom_call_target="Cholesky" | custom-call | tf_op jit(solution)/shard_map/jit(cholesky)/cholesky | solution.py:45
  340.7 10.0 %custom-call.57 = f32[1,128,128]{1,2,0:T(8,128)S(1)} custom-call(f32[1,128,128]{2,1,0:T(8,128)S(1)} %get-tuple-element.52), custom_call_target="InvertDiagBlocksLowerTriangular" | custom-call | tf_op jit(solution)/shard_map/jit(cholesky)/cholesky | solution.py:45
  354.3 13.2 %cholesky.411 = f32[128,128]{1,0:T(8,128)} custom-call(f32[128,128]{1,0:T(8,128)} %cholesky.511), custom_call_target="Cholesky" | custom-call | tf_op jit(solution)/shard_map/jit(cholesky)/cholesky | solution.py:45
  369.0 11.3 %custom-call.58 = f32[1,128,128]{1,2,0:T(8,128)} custom-call(f32[1,128,128]{2,1,0:T(8,128)} %get-tuple-element.49), custom_call_target="InvertDiagBlocksLowerTriangular" | custom-call | tf_op jit(solution)/shard_map/jit(cholesky)/cholesky | solution.py:45
  383.8 12.9 %cholesky.430 = f32[128,128]{1,0:T(8,128)S(1)} custom-call(f32[128,128]{1,0:T(8,128)} %cholesky.516), custom_call_target="Cholesky" | custom-call | tf_op jit(solution)/shard_map/jit(cholesky)/cholesky | solution.py:45
  397.4 10.6 %custom-call.59 = f32[1,128,128]{1,2,0:T(8,128)S(1)} custom-call(f32[1,128,128]{2,1,0:T(8,128)} %get-tuple-element.46), custom_call_target="InvertDiagBlocksLowerTriangular" | custom-call | tf_op jit(solution)/shard_map/jit(cholesky)/cholesky | solution.py:45
  410.1 11.7 %cholesky.449 = f32[128,128]{1,0:T(8,128)S(1)} custom-call(f32[128,128]{1,0:T(8,128)S(1)} %cholesky.521), custom_call_target="Cholesky" | custom-call | tf_op jit(solution)/shard_map/jit(cholesky)/cholesky | solution.py:45
  422.4 9.8 %custom-call.60 = f32[1,128,128]{1,2,0:T(8,128)S(1)} custom-call(f32[1,128,128]{2,1,0:T(8,128)S(1)} %get-tuple-element.43), custom_call_target="InvertDiagBlocksLowerTriangular" | custom-call | tf_op jit(solution)/shard_map/jit(cholesky)/cholesky | solution.py:45
  434.1 11.9 %cholesky.469 = f32[128,128]{1,0:T(8,128)S(1)} custom-call(f32[128,128]{1,0:T(8,128)S(1)} %cholesky.526), custom_call_target="Cholesky" | custom-call | tf_op jit(solution)/shard_map/jit(cholesky)/cholesky | solution.py:45
  446.0 9.8 %custom-call.61 = f32[1,128,128]{1,2,0:T(8,128)S(1)} custom-call(f32[1,128,128]{2,1,0:T(8,128)S(1)} %get-tuple-element.40), custom_call_target="InvertDiagBlocksLowerTriangular" | custom-call | tf_op jit(solution)/shard_map/jit(cholesky)/cholesky | solution.py:45
  458.0 11.7 %cholesky.487 = f32[128,128]{1,0:T(8,128)S(1)} custom-call(f32[128,128]{1,0:T(8,128)S(1)} %convolution_subtract_fusion.14), custom_call_target="Cholesky" | custom-call | tf_op jit(solution)/shard_map/jit(cholesky)/cholesky | solution.py:45
  480.1 24.9 %while.1 = (s32[]{:T(128)}, f32[896,896]{1,0:T(8,128)}, s32[7,2]{0,1:T(2,128)S(1)}, f32[7,128,128]{2,1,0:T(8,128)}, s32[]{:T(128)}) while((s32[]{:T(128)}, f32[896,896]{1,0:T(8,128)}, s32[7,2]{0,1:T(2,128)S(1)}, f32[7,128,128]{2,1,0:T(8,128)}, s32[]{:T(128)}) %tuple.62), condition=%wide.while_cond, body=%wide.while_body.sunk | while | flops 2 | bytes 132705 | solution.py:11
  504.9 70.7 %custom-call.62 = f32[7,128,128]{1,2,0:T(8,128)} custom-call(f32[7,128,128]{2,1,0:T(8,128)} %get-tuple-element.9), custom_call_target="InvertDiagBlocksLowerTriangular" | custom-call | tf_op jit(solution)/shard_map/triangular_solve | solution.py:11
  624.2 7.1 fusion.30
  631.4 7.6 convolution_bitcast_fusion
  639.1 29.3 %reduce-scatter.3.cloned.1.call-done = f32[512,256]{0,1:T(8,128)} async-done(((f32[2048,256]{0,1:T(8,128)}), f32[512,256]{0,1:T(8,128)}) %reduce-scatter.3.cloned.1.call-update) | async-done | bytes 524304 | tf_op jit(solution)/shard_map/reduce_scatter | solution.py:64
  670.2 54.3 %all-gather.5.cloned.1.call-done = bf16[512,8192]{0,1:T(8,128)(2,1)} async-done(((bf16[512,256]{0,1:T(8,128)(2,1)}), bf16[512,8192]{0,1:T(8,128)(2,1)}) %all-gather.5.cloned.1.call-update) | async-done | bytes 8388624 | tf_op jit(solution)/shard_map/all_gather | solution.py:68
  724.5 7.8 convolution_convert_fusion
  732.4 46.1 %reduce-scatter.5.cloned.1.call-done = bf16[256,2048]{1,0:T(8,128)(2,1)} async-done(((bf16[256,8192]{1,0:T(8,128)(2,1)}), bf16[256,2048]{1,0:T(8,128)(2,1)}) %reduce-scatter.5.cloned.1.call-update) | async-done | bytes 1048592 | tf_op jit(solution)/shard_map/reduce_scatter | solution.py:73
  (185 shorter events, 139.9 us)
Async XLA Ops:
  7.2 14.3 %copy-start = (bf16[256,2048]{1,0:T(8,128)(2,1)S(1)}, bf16[256,2048]{1,0:T(8,128)(2,1)}, u32[]{:S(2)}) copy-start(bf16[256,2048]{1,0:T(8,128)(2,1)} %param.5) | copy-start | bytes 3145732
  7.2 56.9 %all-reduce.5.cloned.1.call-start = ((), (), s32[]{:S(2)}) async-start(), calls=%async_computation.2 | async-start | bytes 1835008 | tf_op jit(solution)/shard_map/psum | solution.py:30
  16.1 0.9 copy-start.10
  17.1 163.9 %all-reduce.9.cloned.1.call-start = ((), (), s32[]{:S(2)}) async-start(), calls=%async_computation.4 | async-start | bytes 7340032 | tf_op jit(solution)/shard_map/psum | solution.py:41
  28.4 265.3 %all-reduce.7.cloned.1.call-start = ((), (), s32[]{:S(2)}) async-start(), calls=%async_computation.3 | async-start | bytes 6422528 | tf_op jit(solution)/shard_map/psum | solution.py:44
  64.1 5.3 copy-start.2
  68.1 4.3 copy-start.12
  70.0 1.7 copy-start.7
  71.7 559.7 %all-gather.3.cloned.1.call-start = ((), (), s32[]{:S(2)}) async-start(), calls=%async_computation.5 | async-start | bytes 8650752 | tf_op jit(solution)/shard_map/all_gather | solution.py:57
  72.3 596.1 %reduce-scatter.3.cloned.1.call-start = ((), (), s32[]{:S(2)}) async-start(), calls=%async_computation.6 | async-start | bytes 2621440 | tf_op jit(solution)/shard_map/reduce_scatter | solution.py:64
  293.7 5.0 copy-start.4
  300.9 1.7 copy-start.6
  327.4 0.7 copy-start.9
  446.0 34.1 %copy-start.13 = (s32[7]{0:T(128)S(1)}, s32[7]{0:T(128)}, u32[]{:S(2)}) copy-start(s32[7]{0:T(128)} %get-tuple-element.76) | copy-start | bytes 88
  504.9 72.6 %copy-start.5 = (f32[896,896]{1,0:T(8,128)S(1)}, f32[896,896]{1,0:T(8,128)}, u32[]{:S(2)}) copy-start(f32[896,896]{1,0:T(8,128)} %get-tuple-element.131) | copy-start | bytes 9633796
  575.7 4.3 copy-start.8
  577.5 7.3 slice-start
  581.1 3.8 slice-start.1
  622.7 1.2 copy-start.1
  622.7 1.5 copy-start.3
  631.3 7.7 copy-start.11
  639.0 85.5 %all-gather.5.cloned.1.call-start = ((), (), s32[]{:S(2)}) async-start(), calls=%async_computation.7 | async-start | bytes 8650752 | tf_op jit(solution)/shard_map/all_gather | solution.py:68
  670.2 108.2 %reduce-scatter.5.cloned.1.call-start = ((), (), s32[]{:S(2)}) async-start(), calls=%async_computation.8 | async-start | bytes 5242880 | tf_op jit(solution)/shard_map/reduce_scatter | solution.py:73
Sparse Core Ops, SparseCore 0:
  17.2 46.8 all-reduce.4
  67.4 113.4 all-reduce.8
  184.4 109.2 all-reduce.6
  295.8 53.2 all-gather.2
  639.1 29.1 reduce-scatter.2
  671.3 53.1 all-gather.4
  732.5 45.8 reduce-scatter.4
where the time goes:
time: 794 us; the launch traced here: 788 us
  waiting for transfers between devices  381 us (48%)
  other arithmetic  254 us (32%)
  matrix products  82.4 us (10%)
  local copies, waits for them, and re-layouts  42.1 us (5%)
  between operations  28.4 us (4%)
    another operation x27, other arithmetic, shards(): chol_lower = jnp.linalg.cholesky(inverse_square)  154 us
    psum x1, waiting for transfers between devices, shards(): lax.psum(jnp.concatenate(weight_parts, axis=0).astype(jnp.bfloat16), 'rows')  109 us
    psum x1, waiting for transfers between devices, shards(): inverse_square = lax.psum(jnp.concatenate(inverse_parts, axis=0), 'rows')  107 us
    another operation x3, other arithmetic, spd_solve(): lax.linalg.triangular_solve(chol_lower, forward, left_side=True, lower=Tr...  74 us
    all_gather x1, waiting for transfers between devices, shards(): lax.all_gather(own_rows, 'rows', axis=1, tiled=True)  54.3 us
    reduce_scatter x1, waiting for transfers between devices, shards(): lax.psum_scatter(gram_term.astype(jnp.bfloat16), 'mp', scatter_dimension=...  46.1 us
    psum x1, waiting for transfers between devices, shards(): columns = lax.psum(jnp.concatenate(col_pieces, axis=1), 'mp')  35.7 us
    reduce_scatter x1, waiting for transfers between devices, shards(): lax.psum_scatter(partial_value, 'mp', scatter_dimension=0, tiled=True)  29.3 us
  transfers between devices with their start and end apart: 7, of which 6 were waited for; matrix products, arithmetic and copies ran while one was open for 44% of the time, Pallas kernels for 0%

commit v1 on v0

--- a/solution.py
+++ b/solution.py
@@ -65,7 +65,9 @@
     ).astype(jnp.bfloat16)
     gram_term = lax.dot_general(
         own_rows,
-        lax.all_gather(own_rows, "rows", axis=1, tiled=True),
+        jnp.concatenate(
+            lax.all_to_all(jnp.stack([own_rows] * lax.axis_size("rows")), "rows", 0, 0), axis=1
+        ),
         (((0,), (0,)), ((), ())),
         preferred_element_type=jnp.float32,
     )

time: 794 us -> 836 us (1.053)
  blocking collectives: 0 us -> 103 us
  waiting for transfers between devices: 381 us -> 324 us
    all_to_all x0 -> x1, blocking collectives: none -> 103 us  [shards(): lax.all_to_all(jnp.stack([own_rows] * lax.axis_size('rows')), 'rows', 0, 0)]
    all_gather x1 -> x0, waiting for transfers between devices: 54.3 us -> none  [shards(): lax.all_gather(own_rows, 'rows', axis=1, tiled=True)]
    another operation x21 -> x22, local copies, waits for them, and re-layouts: 24.9 us -> 25.4 us
  transfers between devices with their start and end apart: 7 -> 6, of which waited for: 6 -> 5; matrix products, arithmetic and copies ran while one was open for 44% -> 42% of each run, Pallas kernels for 0% -> 0%
where the time goes in v1:
time: 836 us; the launch traced here: 830 us
  waiting for transfers between devices  324 us (39%)
  other arithmetic  253 us (30%)
  blocking collectives  103 us (12%)
  matrix products  78.9 us (9%)
  local copies, waits for them, and re-layouts  42.7 us (5%)
  between operations  28.6 us (3%)
    another operation x27, other arithmetic, shards(): chol_lower = jnp.linalg.cholesky(inverse_square)  154 us
    psum x1, waiting for transfers between devices, shards(): lax.psum(jnp.concatenate(weight_parts, axis=0).astype(jnp.bfloat16), 'rows')  109 us
    psum x1, waiting for transfers between devices, shards(): inverse_square = lax.psum(jnp.concatenate(inverse_parts, axis=0), 'rows')  107 us
    all_to_all x1, blocking collectives, shards(): lax.all_to_all(jnp.stack([own_rows] * lax.axis_size('rows')), 'rows', 0, 0)  103 us
    another operation x3, other arithmetic, spd_solve(): lax.linalg.triangular_solve(chol_lower, forward, left_side=True, lower=Tr...  73.9 us
    reduce_scatter x1, waiting for transfers between devices, shards(): lax.psum_scatter(gram_term.astype(jnp.bfloat16), 'mp', scatter_dimension=...  43 us
    psum x1, waiting for transfers between devices, shards(): columns = lax.psum(jnp.concatenate(col_pieces, axis=1), 'mp')  35.5 us
    reduce_scatter x1, waiting for transfers between devices, shards(): lax.psum_scatter(partial_value, 'mp', scatter_dimension=0, tiled=True)  29.3 us
  transfers between devices with their start and end apart: 6, of which 5 were waited for; matrix products, arithmetic and copies ran while one was open for 42% of the time, Pallas kernels for 0%

profile of v1, /device:TPU:1, one launch (start us, length us, event | category | flops | bytes accessed | tf_op | source)
XLA Modules:
  0.0 830.4 jit_solution(15073076830216419069)
XLA Ops:
  28.6 35.5 %all-reduce.5.cloned.1.call-done = f32[256,896]{0,1:T(8,128)} async-done(((f32[256,896]{0,1:T(8,128)}), f32[256,896]{0,1:T(8,128)}) %all-reduce.5.cloned.1.call-update) | async-done | bytes 917520 | tf_op jit(solution)/shard_map/psum | solution.py:30
  72.6 108.5 %all-reduce.9.cloned.1.call-done = bf16[896,2048]{1,0:T(8,128)(2,1)} async-done(((bf16[896,2048]{1,0:T(8,128)(2,1)}), bf16[896,2048]{1,0:T(8,128)(2,1)}) %all-reduce.9.cloned.1.call-update) | async-done | bytes 3670032 | tf_op jit(solution)/shard_map/psum | solution.py:41
  181.1 6.0 convert_element_type.111
  187.1 106.7 %all-reduce.7.cloned.1.call-done = f32[896,896]{0,1:T(8,128)} async-done(((f32[896,896]{0,1:T(8,128)}), f32[896,896]{0,1:T(8,128)}) %all-reduce.7.cloned.1.call-update) | async-done | bytes 3211280 | tf_op jit(solution)/shard_map/psum | solution.py:44
  302.8 11.7 %cholesky.195 = f32[128,128]{1,0:T(8,128)S(1)} custom-call(f32[128,128]{1,0:T(8,128)S(1)} %cholesky.502), custom_call_target="Cholesky" | custom-call | tf_op jit(solution)/shard_map/jit(cholesky)/cholesky | solution.py:45
  314.8 9.8 %custom-call.56 = f32[1,128,128]{1,2,0:T(8,128)S(1)} custom-call(f32[1,128,128]{2,1,0:T(8,128)S(1)} %get-tuple-element.55), custom_call_target="InvertDiagBlocksLowerTriangular" | custom-call | tf_op jit(solution)/shard_map/jit(cholesky)/cholesky | solution.py:45
  328.3 11.7 %cholesky.216 = f32[128,128]{1,0:T(8,128)S(1)} custom-call(f32[128,128]{1,0:T(8,128)S(1)} %cholesky.506), custom_call_target="Cholesky" | custom-call | tf_op jit(solution)/shard_map/jit(cholesky)/cholesky | solution.py:45
  340.7 10.0 %custom-call.57 = f32[1,128,128]{1,2,0:T(8,128)S(1)} custom-call(f32[1,128,128]{2,1,0:T(8,128)S(1)} %get-tuple-element.52), custom_call_target="InvertDiagBlocksLowerTriangular" | custom-call | tf_op jit(solution)/shard_map/jit(cholesky)/cholesky | solution.py:45
  354.3 13.2 %cholesky.411 = f32[128,128]{1,0:T(8,128)} custom-call(f32[128,128]{1,0:T(8,128)} %cholesky.511), custom_call_target="Cholesky" | custom-call | tf_op jit(solution)/shard_map/jit(cholesky)/cholesky | solution.py:45
  369.0 11.3 %custom-call.58 = f32[1,128,128]{1,2,0:T(8,128)} custom-call(f32[1,128,128]{2,1,0:T(8,128)} %get-tuple-element.49), custom_call_target="InvertDiagBlocksLowerTriangular" | custom-call | tf_op jit(solution)/shard_map/jit(cholesky)/cholesky | solution.py:45
  383.9 12.9 %cholesky.430 = f32[128,128]{1,0:T(8,128)S(1)} custom-call(f32[128,128]{1,0:T(8,128)} %cholesky.516), custom_call_target="Cholesky" | custom-call | tf_op jit(solution)/shard_map/jit(cholesky)/cholesky | solution.py:45
  397.4 10.6 %custom-call.59 = f32[1,128,128]{1,2,0:T(8,128)S(1)} custom-call(f32[1,128,128]{2,1,0:T(8,128)} %get-tuple-element.46), custom_call_target="InvertDiagBlocksLowerTriangular" | custom-call | tf_op jit(solution)/shard_map/jit(cholesky)/cholesky | solution.py:45
  410.1 11.7 %cholesky.449 = f32[128,128]{1,0:T(8,128)S(1)} custom-call(f32[128,128]{1,0:T(8,128)S(1)} %cholesky.521), custom_call_target="Cholesky" | custom-call | tf_op jit(solution)/shard_map/jit(cholesky)/cholesky | solution.py:45
  422.4 9.8 %custom-call.60 = f32[1,128,128]{1,2,0:T(8,128)S(1)} custom-call(f32[1,128,128]{2,1,0:T(8,128)S(1)} %get-tuple-element.43), custom_call_target="InvertDiagBlocksLowerTriangular" | custom-call | tf_op jit(solution)/shard_map/jit(cholesky)/cholesky | solution.py:45
  434.1 11.9 %cholesky.469 = f32[128,128]{1,0:T(8,128)S(1)} custom-call(f32[128,128]{1,0:T(8,128)S(1)} %cholesky.526), custom_call_target="Cholesky" | custom-call | tf_op jit(solution)/shard_map/jit(cholesky)/cholesky | solution.py:45
  446.0 9.8 %custom-call.61 = f32[1,128,128]{1,2,0:T(8,128)S(1)} custom-call(f32[1,128,128]{2,1,0:T(8,128)S(1)} %get-tuple-element.40), custom_call_target="InvertDiagBlocksLowerTriangular" | custom-call | tf_op jit(solution)/shard_map/jit(cholesky)/cholesky | solution.py:45
  458.1 11.7 %cholesky.487 = f32[128,128]{1,0:T(8,128)S(1)} custom-call(f32[128,128]{1,0:T(8,128)S(1)} %convolution_subtract_fusion.14), custom_call_target="Cholesky" | custom-call | tf_op jit(solution)/shard_map/jit(cholesky)/cholesky | solution.py:45
  480.3 24.5 %while.1 = (s32[]{:T(128)}, f32[896,896]{1,0:T(8,128)}, s32[7,2]{0,1:T(2,128)S(1)}, f32[7,128,128]{2,1,0:T(8,128)}, s32[]{:T(128)}) while((s32[]{:T(128)}, f32[896,896]{1,0:T(8,128)}, s32[7,2]{0,1:T(2,128)S(1)}, f32[7,128,128]{2,1,0:T(8,128)}, s32[]{:T(128)}) %tuple.62), condition=%wide.while_cond, body=%wide.while_body.sunk | while | flops 2 | bytes 132705 | solution.py:11
  504.8 70.7 %custom-call.62 = f32[7,128,128]{1,2,0:T(8,128)} custom-call(f32[7,128,128]{2,1,0:T(8,128)} %get-tuple-element.9), custom_call_target="InvertDiagBlocksLowerTriangular" | custom-call | tf_op jit(solution)/shard_map/triangular_solve | solution.py:11
  624.1 7.1 fusion.30
  631.2 7.6 convolution_bitcast_fusion
  638.9 29.3 %reduce-scatter.3.cloned.1.call-done = f32[512,256]{0,1:T(8,128)} async-done(((f32[2048,256]{0,1:T(8,128)}), f32[512,256]{0,1:T(8,128)}) %reduce-scatter.3.cloned.1.call-update) | async-done | bytes 524304 | tf_op jit(solution)/shard_map/reduce_scatter | solution.py:64
  670.3 103.0 %all_to_all.5 = bf16[32,512,256]{1,2,0:T(8,128)(2,1)S(1)} all-to-all(bf16[32,512,256]{1,2,0:T(8,128)(2,1)S(1)} %stack.2), channel_id=1, replica_groups=mesh['rows'=32,'mp'=4] {'rows'}, dimensions={0} | all-to-all | bytes 16777216 | tf_op jit(solution)/shard_map/all_to_all | solution.py:69
  777.6 43.0 %reduce-scatter.5.cloned.1.call-done = bf16[256,2048]{1,0:T(8,128)(2,1)} async-done(((bf16[256,8192]{1,0:T(8,128)(2,1)}), bf16[256,2048]{1,0:T(8,128)(2,1)}) %reduce-scatter.5.cloned.1.call-update) | async-done | bytes 1048592 | tf_op jit(solution)/shard_map/reduce_scatter | solution.py:75
  (184 shorter events, 138.2 us)
Async XLA Ops:
  7.2 14.5 %copy-start = (bf16[256,2048]{1,0:T(8,128)(2,1)S(1)}, bf16[256,2048]{1,0:T(8,128)(2,1)}, u32[]{:S(2)}) copy-start(bf16[256,2048]{1,0:T(8,128)(2,1)} %param.5) | copy-start | bytes 3145732
  7.2 57.0 %all-reduce.5.cloned.1.call-start = ((), (), s32[]{:S(2)}) async-start(), calls=%async_computation.3 | async-start | bytes 1835008 | tf_op jit(solution)/shard_map/psum | solution.py:30
  16.2 0.9 copy-start.10
  17.2 163.9 %all-reduce.9.cloned.1.call-start = ((), (), s32[]{:S(2)}) async-start(), calls=%async_computation.5 | async-start | bytes 7340032 | tf_op jit(solution)/shard_map/psum | solution.py:41
  28.6 265.2 %all-reduce.7.cloned.1.call-start = ((), (), s32[]{:S(2)}) async-start(), calls=%async_computation.4 | async-start | bytes 6422528 | tf_op jit(solution)/shard_map/psum | solution.py:44
  64.2 5.3 copy-start.2
  68.2 4.3 copy-start.12
  70.1 1.7 copy-start.7
  71.8 559.4 %all-gather.2.cloned.1.call-start = ((), (), s32[]{:S(2)}) async-start(), calls=%async_computation.6 | async-start | bytes 8650752 | tf_op jit(solution)/shard_map/all_gather | solution.py:57
  72.4 595.8 %reduce-scatter.3.cloned.1.call-start = ((), (), s32[]{:S(2)}) async-start(), calls=%async_computation.7 | async-start | bytes 2621440 | tf_op jit(solution)/shard_map/reduce_scatter | solution.py:64
  293.8 5.0 copy-start.4
  301.1 1.7 copy-start.6
  327.5 0.7 copy-start.9
  446.0 34.3 %copy-start.13 = (s32[7]{0:T(128)S(1)}, s32[7]{0:T(128)}, u32[]{:S(2)}) copy-start(s32[7]{0:T(128)} %get-tuple-element.76) | copy-start | bytes 88
  504.8 72.6 %copy-start.5 = (f32[896,896]{1,0:T(8,128)S(1)}, f32[896,896]{1,0:T(8,128)}, u32[]{:S(2)}) copy-start(f32[896,896]{1,0:T(8,128)} %get-tuple-element.130) | copy-start | bytes 9633796
  575.5 4.3 copy-start.8
  577.4 7.3 slice-start
  580.9 3.8 slice-start.1
  622.6 1.2 copy-start.1
  622.6 1.5 copy-start.3
  631.2 7.7 copy-start.11
  638.9 181.7 %reduce-scatter.5.cloned.1.call-start = ((), (), s32[]{:S(2)}) async-start(), calls=%async_computation.8 | async-start | bytes 5242880 | tf_op jit(solution)/shard_map/reduce_scatter | solution.py:75
Sparse Core Ops, SparseCore 0:
  17.3 46.8 all-reduce.4
  67.6 113.4 all-reduce.8
  184.5 109.2 all-reduce.6
  295.9 53.2 all-gather.1
  639.0 29.1 reduce-scatter.2
  777.7 42.8 reduce-scatter.4
